TPU v7x, 256 devices: a whole 4x4x8 slice. The times are simulated.
256 devices in a mesh: seq: 32 (over x, y, core), head: 8 (over z).
Axes of the slice: x: 4, y: 4, z: 8, core: 2. Of those that a mesh axis runs over, the one named last changes fastest.
Arguments:
- queries: bfloat16 [2048, 64, 192], P('seq', 'head'), may hold values from -16 to 16
- span_latent: bfloat16 [2048, 576], P('seq'), may hold values from -4 to 4
- cache_latent: bfloat16 [2048, 576], P('seq'), may hold values from -4 to 4
- segments: int32 [2048], replicated, may hold values from 0 to 3, never falling along the last dimension, each value on 1 to 1024 neighbouring positions
- prefix_len: int32 [1], replicated, may hold values from 64 to 2048
- w_uk: bfloat16 [64, 128, 512], P('head'), may hold values from -0.25 to 0.25
- value_up_weight: bfloat16 [64, 512, 128], P('head'), may hold values from -0.5 to 0.5
- w_out: bfloat16 [8192, 7168], P('head', 'seq'), may hold values from -0.25 to 0.25
Outputs:
- attended: bfloat16 [2048, 7168], P('seq', 'head')
All inputs are finite; a program needn't handle non-finite values.
Results may differ from a plain program's by a relative error of at most 0.014.
Values may be sent and summed in bfloat16 or wider, within the bound.
A program may use at most 128 MiB of HBM per device.

v0:
```python
import math

import jax
import jax.numpy as jnp
from jax import lax
from jax.sharding import PartitionSpec as P


def on_device(
    queries, span_latent, cache_latent, segments, prefix_len, w_uk, value_up_weight, w_out
):
    tok_rows = queries.shape[0]
    head_count = queries.shape[1]
    nope_width = w_uk.shape[1]
    latent_width = w_uk.shape[2]
    rope_width = queries.shape[2] - nope_width
    value_width = value_up_weight.shape[2]
    scaling = 1.0 / math.sqrt(nope_width + rope_width)
    query_latent = jnp.einsum(
        "thn,hnk->thk", queries[:, :, :nope_width], w_uk, preferred_element_type=jnp.float32
    ).astype(jnp.bfloat16)
    query_full = jnp.concatenate([query_latent, queries[:, :, nope_width:]], axis=2)
    query_full = query_full.reshape(tok_rows * head_count, latent_width + rope_width)
    first_row = lax.axis_index("seq") * tok_rows
    row_position = jnp.repeat(first_row + jnp.arange(tok_rows, dtype=jnp.int32), head_count)
    row_segment = jnp.repeat(lax.dynamic_slice_in_dim(segments, first_row, tok_rows), head_count)
    prefix_end = prefix_len[0]
    row_total = tok_rows * head_count
    cache_portion = lax.all_gather(cache_latent, "seq", axis=0, tiled=True)
    span_piece = lax.all_gather(span_latent, "seq", axis=0, tiled=True)
    key_count = cache_portion.shape[0]
    key_position = jnp.arange(key_count, dtype=jnp.int32)
    see_cache = (row_segment[:, None] == 0) & (key_position[None, :] < prefix_end)
    see_span = (row_segment[:, None] == segments[None, :]) & (
        key_position[None, :] <= row_position[:, None]
    )
    visible = jnp.concatenate([see_cache, see_span], axis=1)
    key_rows = jnp.concatenate([cache_portion, span_piece], axis=0)
    running_max = jnp.full((row_total,), -1e30, jnp.float32)
    logit_scores = (
        lax.dot_general(
            query_full, key_rows, (((1,), (1,)), ((), ())), preferred_element_type=jnp.float32
        )
        * scaling
    )
    logit_scores = jnp.where(visible, logit_scores, jnp.float32(-1e30))
    new_max = jnp.maximum(running_max, jnp.max(logit_scores, axis=1))
    expo = jnp.where(visible, jnp.exp(logit_scores - new_max[:, None]), jnp.float32(0.0))
    new_sum = jnp.sum(expo, axis=1)
    new_acc = jnp.dot(
        expo.astype(jnp.bfloat16), key_rows[:, :latent_width], preferred_element_type=jnp.float32
    )
    blended_latent = (
        (new_acc / new_sum[:, None])
        .astype(jnp.bfloat16)
        .reshape(tok_rows, head_count, latent_width)
    )
    head_split = jnp.einsum(
        "mwi,wie->mwe", blended_latent, value_up_weight, preferred_element_type=jnp.float32
    ).astype(jnp.bfloat16)
    head_split = head_split.reshape(tok_rows, head_count * value_width)
    head_input = jnp.dot(
        head_split,
        lax.all_gather(w_out, "seq", axis=1, tiled=True),
        preferred_element_type=jnp.float32,
    )
    summed = lax.psum_scatter(
        head_input.astype(jnp.bfloat16), "head", scatter_dimension=1, tiled=True
    )
    return summed


def solution(mesh):
    placed = (
        P("seq", "head", None),
        P("seq", None),
        P("seq", None),
        P(),
        P(),
        P("head", None, None),
        P("head", None, None),
        P("head", "seq"),
    )
    return jax.shard_map(
        on_device, mesh=mesh, in_specs=placed, out_specs=P("seq", "head"), check_vma=False
    )
```

profile of v0, /device:TPU:4, one launch (start us, length us, event | category | flops | bytes accessed | tf_op | source)
XLA Modules:
  0.0 249.6 jit_solution(4027849361280293158)
XLA Ops:
  6.5 0.0 copy-start
  6.5 0.0 all-gather.4.cloned.1.call-start
  6.5 0.7 all-gather.4.cloned.1.call-update
  7.3 0.0 all-gather.6.cloned.1.call-start
  7.3 0.7 all-gather.6.cloned.1.call-update
  8.0 0.0 all-gather.8.cloned.1.call-start
  8.1 0.7 all-gather.8.cloned.1.call-update
  8.7 0.0 reduce-scatter.4.cloned.1.call-start
  8.8 0.9 slice.9
  9.7 0.9 slice.10
  10.6 0.8 dynamic_slice.3
  11.4 0.1 broadcast_in_dim.21
  11.5 0.1 broadcast_in_dim_reshape.2
  11.6 0.1 broadcast_in_dim.22
  11.7 0.1 le.16
  12.4 0.0 copy-done
  12.5 0.3 fusion.11
  12.8 1.0 pad_maximum_fusion
  13.7 2.7 %fusion.10 = (pred[512,2048]{1,0:T(32,128)(4,1)S(1)}, pred[512,2048]{1,0:T(32,128)(4,1)S(1)}) fusion(s32[512]{0:T(512)S(1)} %le.16, s32[2048]{0:T(1024)} %param.11, s32[512]{0:T(512)S(1)} %broadcast_in_dim_reshape.2, pred[2048]{0:T(1024)(128)(4,1)S(1)} %iota_compare_fusion.1, pred[512]{0:T(512)(128)(4,1)S(1)} %broadcast_compare_fusion), kind=kLoop, calls=%fused_computation.14 | loop fusion | flops 4194304 | bytes 2112000 | tf_op jit(solution)/shard_map/and | solution.py:34
  16.4 45.5 %all-gather.4.cloned.1.call-done = bf16[2048,576]{1,0:T(8,128)(2,1)} async-done(((bf16[64,576]{1,0:T(8,128)(2,1)}), bf16[2048,576]{1,0:T(8,128)(2,1)}) %all-gather.4.cloned.1.call-update) | async-done | bytes 2359312 | tf_op jit(solution)/shard_map/all_gather | solution.py:29
  61.9 3.4 %constant_dynamic-update-slice_fusion.1 = bf16[4096,576]{1,0:T(8,128)(2,1)} fusion(bf16[2048,576]{1,0:T(8,128)(2,1)} %all-gather.4.cloned.1.call-done), kind=kLoop, calls=%fused_computation.32 | loop fusion | bytes 4980736
  65.4 48.1 %all-gather.6.cloned.1.call-done = bf16[2048,576]{1,0:T(8,128)(2,1)} async-done(((bf16[64,576]{1,0:T(8,128)(2,1)}), bf16[2048,576]{1,0:T(8,128)(2,1)}) %all-gather.6.cloned.1.call-update) | async-done | bytes 2359312 | tf_op jit(solution)/shard_map/all_gather | solution.py:30
  113.4 0.0 copy-start.3
  113.4 3.5 %constant_dynamic-update-slice_fusion = bf16[4096,576]{1,0:T(8,128)(2,1)} fusion(bf16[4096,576]{1,0:T(8,128)(2,1)} %constant_dynamic-update-slice_fusion.1, bf16[2048,576]{1,0:T(8,128)(2,1)} %all-gather.6.cloned.1.call-done), kind=kLoop, calls=%fused_computation.31 | loop fusion | bytes 5242880 | tf_op jit(solution)/shard_map/concatenate | solution.py:38
  116.9 0.0 copy-done.3
  116.9 6.7 %fusion = (f32[512]{0:T(512)S(1)}, f32[512,4096]{1,0:T(8,128)S(1)}) fusion(pred[512,2048]{1,0:T(32,128)(4,1)S(1)} %get-tuple-element.7, pred[512,2048]{1,0:T(32,128)(4,1)S(1)} %get-tuple-element.8, bf16[4096,576]{1,0:T(8,128)(2,1)} %constant_dynamic-update-slice_fusion, bf16[64,8,576]{2,0,1:T(8,128)(2,1)S(1)} %copy-done.3), kind=kOutput, calls=%fused_computation.4 | convolution fusion | flops 2424307200 | bytes 15796224 | tf_op jit(solution)/shard_map/dot_general | solution.py:41
  123.7 0.0 copy-start.1
  123.7 2.8 %fusion.1 = f32[512]{0:T(512)S(1)} fusion(f32[512,4096]{1,0:T(8,128)S(1)} %get-tuple-element.6, f32[512]{0:T(512)S(1)} %broadcast_maximum_fusion, pred[512,2048]{1,0:T(32,128)(4,1)S(1)} %get-tuple-element.7, pred[512,2048]{1,0:T(32,128)(4,1)S(1)} %get-tuple-element.8), kind=kLoop, calls=%fused_computation.5 | loop fusion | flops 12582400 | bytes 10489856 | tf_op jit(solution)/shard_map/reduce_sum | solution.py:49
  126.5 0.0 copy-done.1
  126.5 0.0 copy-start.2
  126.5 2.7 %fusion.17 = bf16[64,8,512]{2,1,0:T(8,128)(2,1)S(1)} fusion(bf16[4096,576]{1,0:T(8,128)(2,1)S(1)} %copy-done.1, f32[512,4096]{1,0:T(8,128)S(1)} %get-tuple-element.6, f32[512]{0:T(512)S(1)} %broadcast_maximum_fusion, f32[512]{0:T(512)S(1)} %fusion.1, pred[512,2048]{1,0:T(32,128)(4,1)S(1)} %get-tuple-element.7, pred[512,2048]{1,0:T(32,128)(4,1)S(1)} %get-tuple-element.8), kind=kOutput, calls=%fused_computation.21 | convolution fusion | flops 2160590848 | bytes 15208448 | tf_op jit(solution)/shard_map/dot_general | solution.py:50
  129.2 0.0 copy-done.2
  129.2 0.4 fusion.12
  129.6 59.1 %all-gather.8.cloned.1.call-done = bf16[1024,7168]{0,1:T(8,128)(2,1)} async-done(((bf16[1024,224]{0,1:T(8,128)(2,1)}), bf16[1024,7168]{0,1:T(8,128)(2,1)}) %all-gather.8.cloned.1.call-update) | async-done | bytes 14680080 | tf_op jit(solution)/shard_map/all_gather | solution.py:64
  188.7 9.7 %convolution_convert_fusion = bf16[64,7168]{1,0:T(8,128)(2,1)S(1)} fusion(bf16[1024,7168]{0,1:T(8,128)(2,1)} %all-gather.8.cloned.1.call-done, bf16[8,8,8,128]{3,2,1,0:T(8,128)(2,1)S(1)} %fusion.12), kind=kOutput, calls=%fused_computation.3 | convolution fusion | flops 939982848 | bytes 15728640 | tf_op jit(solution)/shard_map/dot_general | solution.py:62
  198.4 1.7 copy.22
  200.1 0.0 reduce-scatter.4.cloned.1.call-update
  200.1 41.2 %reduce-scatter.4.cloned.1.call-done = bf16[896,64]{1,0:T(8,128)(2,1)} async-done(((bf16[7168,64]{1,0:T(8,128)(2,1)}), bf16[896,64]{1,0:T(8,128)(2,1)}) %reduce-scatter.4.cloned.1.call-update) | async-done | bytes 114704
  241.4 1.7 copy.23
  (5 shorter events, 0.0 us)
Async XLA Ops:
  6.5 5.9 %copy-start = (bf16[8,128,512]{2,1,0:T(8,128)(2,1)S(1)}, bf16[8,128,512]{2,1,0:T(8,128)(2,1)}, u32[]{:S(2)}) copy-start(bf16[8,128,512]{2,1,0:T(8,128)(2,1)} %param.13) | copy-start | bytes 3145732
  6.5 55.4 %all-gather.4.cloned.1.call-start = ((), (), s32[]{:S(2)}) async-start(), calls=%async_computation.1 | async-start | bytes 2703360 | tf_op jit(solution)/shard_map/all_gather | solution.py:29
  7.3 106.2 %all-gather.6.cloned.1.call-start = ((), (), s32[]{:S(2)}) async-start(), calls=%async_computation.2 | async-start | bytes 2703360 | tf_op jit(solution)/shard_map/all_gather | solution.py:30
  8.0 180.7 %all-gather.8.cloned.1.call-start = ((), (), s32[]{:S(2)}) async-start(), calls=%async_computation.3 | async-start | bytes 15138816 | tf_op jit(solution)/shard_map/all_gather | solution.py:64
  8.7 232.6 %reduce-scatter.4.cloned.1.call-start = ((), (), s32[]{:S(2)}) async-start(), calls=%async_computation.4 | async-start | bytes 2064384
  113.4 3.5 %copy-start.3 = (bf16[64,8,576]{2,0,1:T(8,128)(2,1)S(1)}, bf16[64,8,576]{2,0,1:T(8,128)(2,1)}, u32[]{:S(2)}) copy-start(bf16[64,8,576]{2,0,1:T(8,128)(2,1)} %pad_maximum_fusion) | copy-start | bytes 1769476
  123.7 2.8 %copy-start.1 = (bf16[4096,576]{1,0:T(8,128)(2,1)S(1)}, bf16[4096,576]{1,0:T(8,128)(2,1)}, u32[]{:S(2)}) copy-start(bf16[4096,576]{1,0:T(8,128)(2,1)} %constant_dynamic-update-slice_fusion) | copy-start | bytes 14155780
  126.5 2.7 %copy-start.2 = (bf16[8,512,128]{2,1,0:T(8,128)(2,1)S(1)}, bf16[8,512,128]{2,1,0:T(8,128)(2,1)}, u32[]{:S(2)}) copy-start(bf16[8,512,128]{2,1,0:T(8,128)(2,1)} %param.14) | copy-start | bytes 3145732
Sparse Core Ops, SparseCore 0:
  9.9 51.9 all-gather.3
  64.5 48.9 all-gather.5
  116.0 72.6 all-gather.7
  200.2 41.0 reduce-scatter.3
where the time goes:
time: 250 us
  waiting for transfers between devices  196 us (78%)
  matrix products  19.8 us (8%)
  between operations  13.9 us (6%)
  local copies, waits for them, and re-layouts  13.3 us (5%)
  other arithmetic  6.46 us (3%)
    all_gather x1, waiting for transfers between devices, on_device(): lax.all_gather(w_out, 'seq', axis=1, tiled=True)  59.1 us
    all_gather x1, waiting for transfers between devices, on_device(): span_piece = lax.all_gather(span_latent, 'seq', axis=0, tiled=True)  48.1 us
    all_gather x1, waiting for transfers between devices, on_device(): cache_portion = lax.all_gather(cache_latent, 'seq', axis=0, tiled=True)  45.5 us
    unnamed x5, waiting for transfers between devices  43.4 us
    dot_general x1, matrix products, on_device(): jnp.dot(head_split, lax.all_gather(w_out, 'seq', axis=1, tiled=True), pre...  9.72 us
    unnamed x12, local copies, waits for them, and re-layouts  6.86 us
    dot_general x1, matrix products, on_device(): lax.dot_general(query_full, key_rows, (((1,), (1,)), ((), ())), preferred...  6.7 us
  transfers between devices with their start and end apart: 4, of which 4 were waited for; matrix products, arithmetic and copies ran while one was open for 11% of the time, Pallas kernels for 0%

commit v1 on v0

v1 whole, which is shorter than its diff:
```python
import functools
import math

import jax
import jax.numpy as jnp
from jax import lax
from jax.experimental import pallas as pl
from jax.experimental.pallas import tpu as pltpu
from jax.sharding import PartitionSpec as P

MESH = pl.DeviceIdType.MESH
F32 = jnp.float32
BF16 = jnp.bfloat16

SIDE = 4
CHIPS = 16
CORES = 2
DEPTH = 8
TOK = 64
HEADS = 8
NOPE = 128
ROPE = 64
LAT = 512
VD = 128
COLS = 224
ROWS = HEADS * CORES * TOK
TILE = 256
KEYS = SIDE * TOK
LOW = -1e30
MASKED = -2e30

A, B, WHOLE = (0, 32), (32, 32), (0, 64)
Q = [(0, 16), (16, 16), (32, 16), (48, 16)]


def _events():
    ev = [
        (0, 0, WHOLE, 0, 1),
        (0, 0, WHOLE, 0, 3),
        (0, 0, WHOLE, 1, 0),
        (0, 0, WHOLE, 3, 0),
        (0, 3, A, 0, 1),
        (0, 1, B, 0, 3),
        (3, 0, A, 1, 0),
        (1, 0, B, 3, 0),
    ]
    for dy in (3, 1, 2):
        ev += [(0, dy, A, 1, 0), (0, dy, A, 3, 0)]
    for dx in (3, 1, 2):
        ev += [(dx, 0, B, 0, 1), (dx, 0, B, 0, 3)]
    for dy in (3, 1, 2):
        ev += [(3, dy, Q[0], 1, 0), (1, dy, Q[1], 3, 0)]
    for dx in (3, 1, 2):
        ev += [(dx, 3, Q[2], 0, 1), (dx, 1, Q[3], 0, 3)]
    return ev


EVENTS = _events()


def kernel(
    q_ref, span_ref, cache_ref, seg_ref, pre_ref, wuk_hbm, vup_hbm, wo_hbm, out_ref,
    kv, qs, qf, m_ref, l_ref, acc, bias, wuk, vup, wo, pp, pr, pha, part, sp, rp, fs, fr,
    g1s, g1r, g2s, g2r, loc, sibs, sibr, rss, rsr, fss, fsr,
):
    s = lax.axis_index("seq")
    z = lax.axis_index("head")
    c = lax.rem(s, CORES)
    chip = s // CORES
    x = chip // SIDE
    y = lax.rem(chip, SIDE)

    def wrap(v, n):
        return lax.rem(v + n, n)

    def at(dx, dy):
        return wrap(x + dx, SIDE) * SIDE + wrap(y + dy, SIDE)

    def device(dx, dy):
        return (at(dx, dy) * CORES + c, z)

    sibling = (chip * CORES + 1 - c, z)
    up = (s, wrap(z + 1, DEPTH))
    down = (s, wrap(z + DEPTH - 1, DEPTH))

    target_head = 2 * x + y // 2

    def target(u):
        return ((wrap(x + u, SIDE) * SIDE + z // 2) * CORES + c, target_head)

    at_home = jnp.logical_and(y == z // 2, target_head == z)
    away = jnp.logical_not(at_home)

    barrier = pltpu.get_barrier_semaphore()
    near = [device(0, 1), device(0, 3), device(1, 0), device(3, 0), sibling, up, down]
    for dev in near:
        pl.semaphore_signal(barrier, inc=1, device_id=dev, device_id_type=MESH)
    home_x = z // 2
    home_y = 2 * lax.rem(z, 2)

    copies = [
        pltpu.make_async_copy(wuk_hbm, wuk, loc.at[0]),
        pltpu.make_async_copy(vup_hbm, vup, loc.at[1]),
        pltpu.make_async_copy(wo_hbm, wo.at[c], loc.at[2]),
    ]
    for cp in copies:
        cp.start()
    kv[chip, :, 0:LAT] = cache_ref[:, 0:LAT]
    kv[chip, :, LAT : 2 * LAT] = span_ref[:, 0:LAT]
    kv[chip, :, 2 * LAT : 2 * LAT + 2 * ROPE] = jnp.concatenate(
        [cache_ref[:, LAT:], span_ref[:, LAT:]], axis=1
    )

    pl.semaphore_wait(barrier, len(near))

    class Gather:
        def __init__(self, buf, send, recv):
            self.buf, self.send, self.recv = buf, send, recv

        def _copy(self, k, dx, dy, rows, sx, sy):
            ref = self.buf.at[at(dx, dy), pl.ds(rows[0], rows[1])]
            return pltpu.make_async_remote_copy(
                src_ref=ref, dst_ref=ref, send_sem=self.send.at[k], recv_sem=self.recv.at[k],
                device_id=device(sx, sy), device_id_type=MESH,
            )

        def start(self, *ks):
            for k in ks:
                self._copy(k, *EVENTS[k]).start()

        def wait(self, *ks):
            for k in ks:
                dx, dy, rows, sx, sy = EVENTS[k]
                self._copy(k, (dx - sx) % 4, (dy - sy) % 4, rows, sx, sy).wait_recv()

        def done(self):
            for k in range(len(EVENTS)):
                self._copy(k, *EVENTS[k]).wait_send()

        def run(self, on_line):
            self.start(0, 1, 2, 3)
            yield
            for got, sends in (
                (0, (4, 8, 9)), (1, (5, 10, 11)), (2, (6, 14, 15)), (3, (7, 16, 17)),
                (4, (12, 13)), (7, (18, 19)),
                (8, (20,)), (9, (21,)), (10, (22,)), (11, (23,)),
                (14, (26,)), (15, (27,)), (16, (28,)), (17, (29,)),
            ):
                self.wait(got)
                self.start(*sends)
            self.wait(5)
            on_line(0)
            for got, sends in ((12, (24,)), (13, (25,)), (18, (30,)), (19, (31,))):
                self.wait(got)
                self.start(*sends)
            self.wait(26, 27)
            on_line(3)
            self.wait(28, 29)
            on_line(1)
            self.wait(6, 20, 21, 22, 23, 24, 25, 30, 31)
            on_line(2)
            yield

    def to_sibling(src, dst, k):
        return pltpu.make_async_remote_copy(
            src_ref=src, dst_ref=dst, send_sem=sibs.at[k], recv_sem=sibr.at[k],
            device_id=sibling, device_id_type=MESH,
        )

    q_swap = to_sibling(q_ref, qs, 0)
    span_len = CHIPS * CORES * TOK
    token = (chip * (CORES * TOK) + lax.broadcasted_iota(jnp.int32, (CORES * TOK, 1), 0)).astype(F32)
    segs = seg_ref[...]
    firsts = [
        jnp.sum(jnp.sum((segs < k).astype(F32), axis=1, keepdims=True), axis=0, keepdims=True)
        for k in (1, 2, 3)
    ]
    start_of = jnp.zeros_like(token)
    for first in firsts:
        start_of = jnp.maximum(start_of, jnp.where(token >= first, first, 0.0))
    prefix = pre_ref[0].astype(F32)
    cache_end = jnp.where(token < firsts[0], prefix - 1.0, -1.0)
    exponent = math.log2(math.e) / math.sqrt(NOPE + ROPE)

    def attend(kind, dx):
        line = wrap(x + dx, SIDE)
        base = line * SIDE
        k_lat = kv[pl.ds(base, SIDE), :, kind * LAT : (kind + 1) * LAT].reshape(KEYS, LAT)
        k_rope = kv[pl.ds(base, SIDE), :, 2 * LAT : 2 * LAT + 2 * ROPE].reshape(KEYS, 2 * ROPE)
        lane = lax.broadcasted_iota(jnp.int32, (1, KEYS), 1)
        pos = (line * (SIDE * CORES * TOK) + (lane // TOK) * (CORES * TOK) + c * TOK + lax.rem(lane, TOK)).astype(F32)
        if kind == 0:
            seen = pos <= cache_end
        else:
            seen = jnp.logical_and(pos >= start_of, pos <= token)
        bias[...] = jnp.where(seen, 0.0, MASKED)

        def tile(i, carry):
            rows = pl.ds(pl.multiple_of(i * TILE, TILE), TILE)
            nt = (((1,), (1,)), ((), ()))
            sc = lax.dot_general(qf[rows, 0:LAT], k_lat, nt, preferred_element_type=F32)
            sc += lax.dot_general(
                qf[rows, LAT + kind * 2 * ROPE : LAT + (kind + 1) * 2 * ROPE], k_rope, nt,
                preferred_element_type=F32,
            )
            both = bias[...]
            sc = sc + jnp.concatenate([both, both], axis=0)
            m_old = m_ref[rows, :]
            m_new = jnp.maximum(m_old, jnp.max(sc, axis=1, keepdims=True))
            shrink = jnp.exp2((m_old - m_new) * exponent)
            p = jnp.exp2((sc - jnp.concatenate([m_new, m_new], axis=1)) * exponent)
            l_ref[rows, :] = l_ref[rows, :] * shrink + (p[:, 0:128] + p[:, 128:256])
            acc[rows, :] = acc[rows, :] * jnp.concatenate([shrink] * 4, axis=1) + jnp.dot(
                p.astype(BF16), k_lat, preferred_element_type=F32
            )
            m_ref[rows, :] = m_new
            return carry

        lax.fori_loop(0, ROWS // TILE, tile, 0, unroll=2)

    def keys_line(dx):
        if dx == 0:
            lift_queries()

        @pl.when(x < 2)
        def _():
            attend(0, dx)

        if dx == 0:
            attend(1, 0)
        elif dx == 3:

            @pl.when(x >= 1)
            def _():
                attend(1, 3)

        elif dx == 2:

            @pl.when(x >= 2)
            def _():
                attend(1, 2)

    def lift_queries():
        m_ref[...] = jnp.full_like(m_ref, LOW)
        l_ref[...] = jnp.zeros_like(l_ref)
        acc[...] = jnp.zeros_like(acc)
        copies[0].wait()
        row = lax.broadcasted_iota(jnp.int32, (HEADS * TOK, HEADS * TOK), 0)
        col = lax.broadcasted_iota(jnp.int32, (HEADS * TOK, HEADS * TOK), 1)
        order = (col == lax.rem(row, TOK) * HEADS + row // TOK).astype(BF16)
        nothing = jnp.zeros((TOK, ROPE), BF16)
        for src, core in ((q_ref, c), (qs, 1 - c)):
            if core is not c:
                q_swap.wait_recv()
            qp = jnp.dot(order, src[...], preferred_element_type=F32).astype(BF16)
            for h in range(HEADS):
                rows = pl.ds(pl.multiple_of(h * (CORES * TOK) + core * TOK, TOK), TOK)
                own = qp[h * TOK : (h + 1) * TOK]
                qf[rows, 0:LAT] = jnp.dot(own[:, 0:NOPE], wuk[h], preferred_element_type=F32).astype(BF16)
                qf[rows, LAT:] = jnp.concatenate([own[:, NOPE:], nothing, nothing, own[:, NOPE:]], axis=1)

    keys = Gather(kv, g1s, g1r)
    g = keys.run(keys_line)
    next(g)
    q_swap.start()
    wo_swap = to_sibling(wo_hbm, wo.at[c], 1)
    wo_swap.start()
    next(g)

    copies[1].wait()
    half = lax.broadcasted_iota(jnp.int32, (CORES * TOK, 128), 1) < 64
    swaps = []
    for t in range(4):
        for h in (2 * t, 2 * t + 1):
            rows = slice(h * CORES * TOK, (h + 1) * CORES * TOK)
            total = jnp.sum(l_ref[rows, :], axis=1, keepdims=True)
            o = (acc[rows, :] / jnp.where(total > 0.0, total, 1.0)).astype(BF16)
            ph = jnp.dot(o, vup[h], preferred_element_type=F32)
            pp[:, h, :, 0:VD] = ph.reshape(CORES, TOK, VD)
            pp[:, h, :, VD:] = jnp.where(half, m_ref[rows, :], total).reshape(CORES, TOK, 128)
        swap = to_sibling(pp.at[1 - c, pl.ds(2 * t, 2)], pr.at[pl.ds(2 * t, 2)], 2 + t)
        swap.start()
        swaps.append(swap)
    for t in range(4):
        swaps[t].wait_recv()
        for h in (2 * t, 2 * t + 1):
            own, other = pp[c, h], pr[h]
            m0, m1 = own[:, VD : VD + 1], other[:, VD : VD + 1]
            l0, l1 = own[:, VD + 64 : VD + 65], other[:, VD + 64 : VD + 65]
            top = jnp.maximum(m0, m1)
            w0 = l0 * jnp.exp2((m0 - top) * exponent)
            w1 = l1 * jnp.exp2((m1 - top) * exponent)
            norm = w0 + w1
            pha[chip, :, h * VD : (h + 1) * VD] = (
                own[:, 0:VD] * (w0 / norm) + other[:, 0:VD] * (w1 / norm)
            ).astype(BF16)

    copies[2].wait()
    to_sibling(wo_hbm, wo.at[1 - c], 1).wait_recv()

    def ring(u, k):
        forth = k < 4
        return pltpu.make_async_remote_copy(
            src_ref=sp.at[u, k], dst_ref=rp.at[u, k], send_sem=rss.at[u * 7 + k],
            recv_sem=rsr.at[u * 7 + k], device_id=up if forth else down, device_id_type=MESH,
        )

    def piece(u, j):
        return part[u, :, pl.ds(pl.multiple_of(j * 32, 32), 32), :]

    def step(u, k):
        for e, hop in ((k, z + 4 - k), (4 + k, z - 3 + k)):
            if e > 6:
                continue
            v = piece(u, wrap(hop + DEPTH, DEPTH))
            if k > 0:
                ring(u, e - 1).wait_recv()
                v = v + rp[u, e - 1].astype(F32)
            sp[u, e] = v.astype(BF16)
            ring(u, e).start()

    def home(u):
        return pltpu.make_async_remote_copy(
            src_ref=fs.at[u], dst_ref=fr.at[lax.rem(y, 2), lax.rem(z, 2)], send_sem=fss.at[u],
            recv_sem=fsr.at[lax.rem(y, 2) * 2 + lax.rem(z, 2)], device_id=target(u), device_id_type=MESH,
        )

    def finish(u):
        ring(u, 3).wait_recv()
        ring(u, 6).wait_recv()
        v = piece(u, z) + rp[u, 3].astype(F32) + rp[u, 6].astype(F32)
        fs[u] = v.astype(BF16)
        if u == 0:

            @pl.when(at_home)
            def _():
                fr[lax.rem(y, 2), lax.rem(z, 2)] = fs[u]

            @pl.when(away)
            def _():
                home(u).start()

        else:
            home(u).start()

    def out_line(dx):
        base = wrap(x + dx, SIDE) * SIDE
        rows = pha[pl.ds(base, SIDE)].reshape(SIDE * TOK, HEADS * VD)
        for i in range(CORES):
            part[dx, i] = jnp.dot(rows, wo[i], preferred_element_type=F32)
        step(dx, 0)
        if dx == 3:
            step(0, 1)
        if dx == 1:
            step(0, 2)
            step(3, 1)
        if dx == 2:
            step(0, 3)
            step(1, 1)
            step(3, 2)

    heads = Gather(pha, g2s, g2r)
    for _ in heads.run(out_line):
        pass
    finish(0)
    step(2, 1)
    step(1, 2)
    step(3, 3)
    finish(3)
    step(2, 2)
    step(1, 3)
    finish(1)
    step(2, 3)
    finish(2)

    for a in range(2):
        for b in range(2):
            mine = jnp.logical_and(
                jnp.logical_and(x == home_x, y == home_y + a), z == 2 * y + b
            )

            @pl.when(jnp.logical_not(mine))
            def _(a=a, b=b):
                pltpu.make_async_remote_copy(
                    src_ref=fs.at[0], dst_ref=fr.at[a, b], send_sem=fss.at[0],
                    recv_sem=fsr.at[a * 2 + b], device_id=sibling, device_id_type=MESH,
                ).wait_recv()

    for b in range(2):
        out_ref[b * 32 : (b + 1) * 32, :] = jnp.concatenate(
            [fr[a, b, i] for a in range(2) for i in range(CORES)], axis=1
        )

    keys.done()
    heads.done()
    q_swap.wait_send()
    wo_swap.wait_send()
    for t in range(4):
        swaps[t].wait_send()
    for u in range(4):
        for k in range(7):
            ring(u, k).wait_send()

    @pl.when(away)
    def _():
        home(0).wait_send()

    for u in range(1, 4):
        home(u).wait_send()


def on_device(queries, span_latent, cache_latent, segments, prefix_len, w_uk, value_up_weight, w_out):
    vmem = pl.BlockSpec(memory_space=pltpu.VMEM)
    smem = pl.BlockSpec(memory_space=pltpu.SMEM)
    hbm = pl.BlockSpec(memory_space=pl.ANY)
    dma = pltpu.SemaphoreType.DMA
    return pl.pallas_call(
        kernel,
        out_shape=jax.ShapeDtypeStruct((TOK, CORES * 2 * COLS), BF16),
        in_specs=[vmem, vmem, vmem, vmem, smem, hbm, hbm, hbm],
        out_specs=vmem,
        scratch_shapes=[
            pltpu.VMEM((CHIPS, TOK, 2 * LAT + 2 * ROPE), BF16),
            pltpu.VMEM((HEADS * TOK, NOPE + ROPE), BF16),
            pltpu.VMEM((ROWS, LAT + 4 * ROPE), BF16),
            pltpu.VMEM((ROWS, 128), F32),
            pltpu.VMEM((ROWS, 128), F32),
            pltpu.VMEM((ROWS, LAT), F32),
            pltpu.VMEM((CORES * TOK, KEYS), F32),
            pltpu.VMEM((HEADS, NOPE, LAT), BF16),
            pltpu.VMEM((HEADS, LAT, VD), BF16),
            pltpu.VMEM((CORES, HEADS * VD, COLS), BF16),
            pltpu.VMEM((CORES, HEADS, TOK, 2 * VD), F32),
            pltpu.VMEM((HEADS, TOK, 2 * VD), F32),
            pltpu.VMEM((CHIPS, TOK, HEADS * VD), BF16),
            pltpu.VMEM((4, CORES, SIDE * TOK, COLS), F32),
            pltpu.VMEM((4, 7, CORES, 32, COLS), BF16),
            pltpu.VMEM((4, 7, CORES, 32, COLS), BF16),
            pltpu.VMEM((4, CORES, 32, COLS), BF16),
            pltpu.VMEM((2, 2, CORES, 32, COLS), BF16),
            dma((32,)), dma((32,)), dma((32,)), dma((32,)),
            dma((3,)), dma((6,)), dma((6,)), dma((28,)), dma((28,)), dma((4,)), dma((4,)),
        ],
        compiler_params=pltpu.CompilerParams(
            collective_id=0, has_side_effects=True, vmem_limit_bytes=48 * 1024 * 1024
        ),
        name="prefill",
    )(
        queries.reshape(HEADS * TOK, NOPE + ROPE),
        span_latent,
        cache_latent,
        segments.reshape(CHIPS, CORES * TOK),
        prefix_len,
        w_uk,
        value_up_weight,
        w_out,
    )


def solution(mesh):
    placed = (
        P("seq", "head", None),
        P("seq", None),
        P("seq", None),
        P(),
        P(),
        P("head", None, None),
        P("head", None, None),
        P("head", "seq"),
    )
    return jax.shard_map(
        on_device, mesh=mesh, in_specs=placed, out_specs=P("seq", "head"), check_vma=False
    )
```

time: 250 us -> 90 us (0.36)
  waiting for transfers between devices: 196 us -> 0 us
  Pallas kernels: 0 us -> 84.8 us
  matrix products: 19.8 us -> 0 us
  between operations: 13.9 us -> 0.74 us
  local copies, waits for them, and re-layouts: 13.3 us -> 4.38 us
  other arithmetic: 6.46 us -> 0 us
    all_gather x3 -> x0, waiting for transfers between devices: 153 us -> none  [the longest x1 59.1 us: on_device(): lax.all_gather(w_out, 'seq', axis=1, tiled=True)]
    pallas_call x0 -> x1, Pallas kernels: none -> 84.8 us  [on_device(): pl.pallas_call(kernel, out_shape=jax.ShapeDtypeStruct((TOK, CORES * 2 * C...]
    unnamed x5 -> x0, waiting for transfers between devices: 43.4 us -> none
    dot_general x5 -> x0, matrix products: 19.8 us -> none  [the longest x1 9.72 us: on_device(): jnp.dot(head_split, lax.all_gather(w_out, 'seq', axis=1, tiled=True), pre...]
    concatenate x1 -> x0, local copies, waits for them, and re-layouts: 3.51 us -> none  [on_device(): key_rows = jnp.concatenate([cache_portion, span_piece], axis=0)]
    reduce_sum x1 -> x0, other arithmetic: 2.81 us -> none  [on_device(): new_sum = jnp.sum(expo, axis=1)]
    and x1 -> x0, other arithmetic: 2.66 us -> none  [on_device(): (row_segment[:, None] == segments[None, :]) & (key_position[None, :] <= r...]
    unnamed x12 -> x14, local copies, waits for them, and re-layouts: 6.86 us -> 4.38 us
  transfers between devices with their start and end apart: 4 -> 0, of which waited for: 4 -> 0; matrix products, arithmetic and copies ran while one was open for 11% -> 0% of each run, Pallas kernels for 0% -> 0%
where the time goes in v1:
time: 90 us; the launch traced here: 89.9 us
  Pallas kernels  84.8 us (94%)
  local copies, waits for them, and re-layouts  4.38 us (5%)
    pallas_call x1, Pallas kernels, on_device(): pl.pallas_call(kernel, out_shape=jax.ShapeDtypeStruct((TOK, CORES * 2 * C...  84.8 us
    unnamed x14, local copies, waits for them, and re-layouts  4.38 us

profile of v1, /device:TPU:4, one launch (start us, length us, event | category | flops | bytes accessed | tf_op | source)
XLA Modules:
  0.0 89.9 jit_solution(5897169036530041731)
XLA Ops:
  0.7 0.0 copy-start.2
  0.7 0.0 copy-start.3
  0.7 0.0 copy-start.4
  0.7 0.0 copy-start.5
  0.7 1.3 %copy.9.wo_hbm = bf16[1024,224]{1,0:T(8,128)(2,1)S(1)} copy(bf16[1024,224]{0,1:T(8,128)(2,1)} %param.15) | data formatting | bytes 917504 | tf_op args[7]
  2.0 0.0 copy-done.2
  2.0 0.0 copy-done.3
  2.0 0.0 copy-done.4
  2.0 0.0 copy-done.5
  2.0 0.0 copy-start
  2.0 1.2 %copy-done = bf16[8,128,512]{2,1,0:T(8,128)(2,1)S(1)} copy-done((bf16[8,128,512]{2,1,0:T(8,128)(2,1)S(1)}, bf16[8,128,512]{2,1,0:T(8,128)(2,1)}, u32[]{:S(2)}) %copy-start) | copy-done | bytes 1048600
  3.2 0.0 copy-start.1
  3.2 1.2 %copy-done.1 = bf16[8,512,128]{2,1,0:T(8,128)(2,1)S(1)} copy-done((bf16[8,512,128]{2,1,0:T(8,128)(2,1)S(1)}, bf16[8,512,128]{2,1,0:T(8,128)(2,1)}, u32[]{:S(2)}) %copy-start.1) | copy-done | bytes 1048600
  4.5 84.8 %prefill.1 = bf16[64,896]{1,0:T(8,128)(2,1)S(1)} custom-call(bf16[512,192]{1,0:T(8,128)(2,1)S(1)} %bitcast.2, bf16[64,576]{1,0:T(8,128)(2,1)S(1)} %copy-done.3, bf16[64,576]{1,0:T(8,128)(2,1)S(1)} %copy-done.4, s32[16,128]{1,0:T(8,128)S(1)} %bitcast.3, s32[1]{0:T(128)S(6)} %copy.11.pre_ref, bf16[8,128,512]{2,1,0:T(8,128)(2,1)S(1)} %copy-done, ...), custom_call_target="tpu_custom_call" | custom-call | tf_op jit(solution)/shard_map/prefill/pallas_call | solution.py:417
  89.2 0.6 copy.12
Async XLA Ops:
  0.7 1.3 %copy-start.2 = (bf16[64,8,192]{2,1,0:T(8,128)(2,1)S(1)}, bf16[64,8,192]{2,1,0:T(8,128)(2,1)}, u32[]{:S(2)}) copy-start(bf16[64,8,192]{2,1,0:T(8,128)(2,1)} %param.8) | copy-start | bytes 589828
  0.7 1.3 %copy-start.3 = (bf16[64,576]{1,0:T(8,128)(2,1)S(1)}, bf16[64,576]{1,0:T(8,128)(2,1)}, u32[]{:S(2)}) copy-start(bf16[64,576]{1,0:T(8,128)(2,1)} %span_ref.1) | copy-start | bytes 221188
  0.7 1.3 %copy-start.4 = (bf16[64,576]{1,0:T(8,128)(2,1)S(1)}, bf16[64,576]{1,0:T(8,128)(2,1)}, u32[]{:S(2)}) copy-start(bf16[64,576]{1,0:T(8,128)(2,1)} %cache_ref.1) | copy-start | bytes 221188
  0.7 1.3 %copy-start.5 = (s32[2048]{0:T(1024)S(1)}, s32[2048]{0:T(1024)}, u32[]{:S(2)}) copy-start(s32[2048]{0:T(1024)} %param.11) | copy-start | bytes 24580
  2.0 1.2 %copy-start = (bf16[8,128,512]{2,1,0:T(8,128)(2,1)S(1)}, bf16[8,128,512]{2,1,0:T(8,128)(2,1)}, u32[]{:S(2)}) copy-start(bf16[8,128,512]{2,1,0:T(8,128)(2,1)} %wuk_hbm.1) | copy-start | bytes 3145732
  3.2 1.2 %copy-start.1 = (bf16[8,512,128]{2,1,0:T(8,128)(2,1)S(1)}, bf16[8,512,128]{2,1,0:T(8,128)(2,1)}, u32[]{:S(2)}) copy-start(bf16[8,512,128]{2,1,0:T(8,128)(2,1)} %vup_hbm.1) | copy-start | bytes 3145732

commit v2 on v0

v2 whole, which is shorter than its diff:
```python
import functools
import math

import jax
import jax.numpy as jnp
from jax import lax
from jax.experimental import pallas as pl
from jax.experimental.pallas import tpu as pltpu
from jax.sharding import PartitionSpec as P

MESH = pl.DeviceIdType.MESH
F32 = jnp.float32
BF16 = jnp.bfloat16

SIDE = 4
CHIPS = 16
CORES = 2
DEPTH = 8
TOK = 64
HEADS = 8
NOPE = 128
ROPE = 64
LAT = 512
VD = 128
COLS = 224
ROWS = HEADS * CORES * TOK
TILE = 512
KEYS = SIDE * TOK
LOW = -1e30
MASKED = -2e30

A, B, WHOLE = (0, 32), (32, 32), (0, 64)
Q = [(0, 16), (16, 16), (32, 16), (48, 16)]


def _by_neighbours():
    ev = [
        (0, 0, WHOLE, 0, 1),
        (0, 0, WHOLE, 0, 3),
        (0, 0, WHOLE, 1, 0),
        (0, 0, WHOLE, 3, 0),
        (0, 3, A, 0, 1),
        (0, 1, B, 0, 3),
        (3, 0, A, 1, 0),
        (1, 0, B, 3, 0),
    ]
    for dy in (3, 1, 2):
        ev += [(0, dy, A, 1, 0), (0, dy, A, 3, 0)]
    for dx in (3, 1, 2):
        ev += [(dx, 0, B, 0, 1), (dx, 0, B, 0, 3)]
    for dy in (3, 1, 2):
        ev += [(3, dy, Q[0], 1, 0), (1, dy, Q[1], 3, 0)]
    for dx in (3, 1, 2):
        ev += [(dx, 3, Q[2], 0, 1), (dx, 1, Q[3], 0, 3)]
    return ev


NEAR = _by_neighbours()
NEAR_1 = [(0, (4, 8, 9)), (1, (5, 10, 11)), (2, (6, 14, 15)), (3, (7, 16, 17))]
NEAR_2 = [
    (4, (12, 13)), (7, (18, 19)), (8, (20,)), (9, (21,)), (10, (22,)), (11, (23,)),
    (14, (26,)), (15, (27,)), (16, (28,)), (17, (29,)),
]
NEAR_3 = [(12, (24,)), (13, (25,)), (18, (30,)), (19, (31,))]


def _by_lines():
    ev = [(0, 0, WHOLE, 0, 1), (0, 0, WHOLE, 0, 3), (0, 0, WHOLE, 1, 0), (0, 0, WHOLE, 3, 0)]
    ev += [(0, 0, WHOLE, 0, 2), (0, 0, WHOLE, 2, 0)]
    ev += [(0, dy, A, sx, 0) for dy in (3, 1, 2) for sx in (1, 3, 2)]
    ev += [(dx, 0, B, 0, sy) for dx in (3, 1, 2) for sy in (1, 3, 2)]
    return ev


LINES = _by_lines()
LINES_1 = [
    (0, (6, 7, 8)), (1, (9, 10, 11)), (2, (15, 16, 17)), (3, (18, 19, 20)), (4, (12, 13, 14)), (5, (21, 22, 23)),
]


def kernel(
    q_hbm, span_hbm, cache_hbm, seg_hbm, pre_hbm, wuk_hbm, vup_hbm, wo_hbm, out_ref,
    q_ref, span_ref, cache_ref, seg_ref, pre_ref,
    kv, qs, qf, m_ref, l_ref, acc, bias, wuk, vup, wz, pp, pr, s1, r1, pha, s4, r4, r5,
    g1s, g1r, g2s, g2r, loc, sibs, sibr, wus, wur, wds, wdr, wps, wpr, s1s, s1r, s4s, s4r, s5s, s5r, known,
):
    s = lax.axis_index("seq")
    z = lax.axis_index("head")
    c = lax.rem(s, CORES)
    chip = s // CORES
    x = chip // SIDE
    y = lax.rem(chip, SIDE)

    def wrap(v, n):
        return lax.rem(v + n, n)

    def at(dx, dy):
        return wrap(x + dx, SIDE) * SIDE + wrap(y + dy, SIDE)

    def device(dx, dy):
        return (at(dx, dy) * CORES + c, z)

    sibling = (chip * CORES + 1 - c, z)
    up = (s, wrap(z + 1, DEPTH))
    down = (s, wrap(z + DEPTH - 1, DEPTH))

    copies = [
        pltpu.make_async_copy(src, dst, loc.at[i])
        for i, (src, dst) in enumerate(
            (
                (cache_hbm, cache_ref), (span_hbm, span_ref), (q_hbm, q_ref), (wuk_hbm, wuk),
                (seg_hbm, seg_ref), (pre_hbm, pre_ref), (vup_hbm, vup), (wo_hbm, wz.at[z, c]),
            )
        )
    ]
    for cp in copies:
        cp.start()

    barrier = pltpu.get_barrier_semaphore()
    near = [device(*d) for d in ((0, 1), (0, 3), (1, 0), (3, 0))] + [sibling, up, down]
    for dev in near:
        pl.semaphore_signal(barrier, inc=1, device_id=dev, device_id_type=MESH)

    copies[0].wait()
    copies[1].wait()
    kv[chip, :, 0:LAT] = cache_ref[:, 0:LAT]
    kv[chip, :, LAT : 2 * LAT] = span_ref[:, 0:LAT]
    kv[chip, :, 2 * LAT : 2 * LAT + 2 * ROPE] = jnp.concatenate(
        [cache_ref[:, LAT:], span_ref[:, LAT:]], axis=1
    )
    copies[2].wait()
    pl.semaphore_wait(barrier, len(near))

    def tell(n):
        for dev in (up, down):
            pl.semaphore_signal(known.at[n], inc=1, device_id=dev, device_id_type=MESH)

    def hear(n):
        pl.semaphore_wait(known.at[n], 2)

    tell(0)

    class Gather:
        def __init__(self, buf, send, recv, events, lanes):
            self.buf, self.send, self.recv, self.events, self.lanes = buf, send, recv, events, lanes

        def _copy(self, g, k, dx, dy, rows, sx, sy):
            ref = self.buf.at[at(dx, dy), pl.ds(*rows), pl.ds(*self.lanes[g])]
            n = g * len(self.events) + k
            return pltpu.make_async_remote_copy(
                src_ref=ref, dst_ref=ref, send_sem=self.send.at[n], recv_sem=self.recv.at[n],
                device_id=device(sx, sy), device_id_type=MESH,
            )

        def start(self, g, *ks):
            for k in ks:
                self._copy(g, k, *self.events[k]).start()

        def wait(self, g, *ks):
            for k in ks:
                dx, dy, rows, sx, sy = self.events[k]
                self._copy(g, k, (dx - sx) % 4, (dy - sy) % 4, rows, sx, sy).wait_recv()

        def follow(self, g, steps):
            for got, sends in steps:
                self.wait(g, got)
                self.start(g, *sends)

        def done(self):
            for g in range(len(self.lanes)):
                for k in range(len(self.events)):
                    self._copy(g, k, *self.events[k]).wait_send()

    def to_sibling(src, dst, k):
        return pltpu.make_async_remote_copy(
            src_ref=src, dst_ref=dst, send_sem=sibs.at[k], recv_sem=sibr.at[k],
            device_id=sibling, device_id_type=MESH,
        )

    keys = Gather(kv, g1s, g1r, NEAR, [(0, 2 * LAT + 2 * ROPE)])
    keys.start(0, 0, 1, 2, 3)
    q_swap = to_sibling(q_ref, qs, 0)
    q_swap.start()

    def around(way, i):
        half = i % 2 if i < 6 or way > 0 else 1
        block = wrap(z - way * (i // 2) + DEPTH, DEPTH)
        ref = wz.at[block, c, pl.ds(half * (COLS // 2), COLS // 2)]
        send, recv = (wus, wur) if way > 0 else (wds, wdr)
        return pltpu.make_async_remote_copy(
            src_ref=ref, dst_ref=ref, send_sem=send.at[i], recv_sem=recv.at[i],
            device_id=up if way > 0 else down, device_id_type=MESH,
        )

    def around_landed(way, i):
        half = i % 2 if i < 6 or way > 0 else 1
        block = wrap(z - way * (i // 2 + 1) + DEPTH, DEPTH)
        ref = wz.at[block, c, pl.ds(half * (COLS // 2), COLS // 2)]
        send, recv = (wus, wur) if way > 0 else (wds, wdr)
        pltpu.make_async_remote_copy(
            src_ref=ref, dst_ref=ref, send_sem=send.at[i], recv_sem=recv.at[i],
            device_id=up if way > 0 else down, device_id_type=MESH,
        ).wait_recv()

    def pass_block(d, core):
        ref = wz.at[wrap(z + d + DEPTH, DEPTH), core]
        return pltpu.make_async_remote_copy(
            src_ref=ref, dst_ref=ref, send_sem=wps.at[d % DEPTH], recv_sem=wpr.at[d % DEPTH],
            device_id=sibling, device_id_type=MESH,
        )

    def weights_step(i):
        for way in (1, -1):
            around_landed(way, i)
            if i < 4:
                around(way, i + 2).start()
        if i == 4:
            around(1, 6).start()
        elif i == 5:
            around(-1, 6).start()
        if i % 2 == 1:
            pass_block(i // 2 + 1, c).start()
            pass_block(-(i // 2 + 1), c).start()
        elif i == 6:
            pass_block(4, c).start()

    copies[7].wait()
    for i in range(2):
        around(1, i).start()
        around(-1, i).start()
    pass_block(0, c).start()

    m_ref[...] = jnp.full_like(m_ref, LOW)
    l_ref[...] = jnp.zeros_like(l_ref)
    acc[...] = jnp.zeros_like(acc)
    row = lax.broadcasted_iota(jnp.int32, (HEADS * TOK, HEADS * TOK), 0)
    col = lax.broadcasted_iota(jnp.int32, (HEADS * TOK, HEADS * TOK), 1)
    by_head = (col == lax.rem(row, TOK) * HEADS + row // TOK).astype(BF16)
    copies[3].wait()
    for src, core in ((q_ref, c), (qs, 1 - c)):
        if src is qs:
            q_swap.wait_recv()
        qp = jnp.dot(by_head, src[...], preferred_element_type=F32).astype(BF16)
        for h in range(HEADS):
            rows = pl.ds(pl.multiple_of(h * (CORES * TOK) + core * TOK, TOK), TOK)
            own = qp[h * TOK : (h + 1) * TOK]
            qf[rows, 0:LAT] = jnp.dot(own[:, 0:NOPE], wuk[h], preferred_element_type=F32).astype(BF16)
            qf[rows, LAT:] = jnp.concatenate([own[:, NOPE:], own[:, NOPE:]], axis=1)

    copies[4].wait()
    copies[5].wait()
    token = (chip * (CORES * TOK) + lax.broadcasted_iota(jnp.int32, (CORES * TOK, 1), 0)).astype(F32)
    segs = seg_ref[...]
    firsts = [
        jnp.sum(jnp.sum((segs < k).astype(F32), axis=1, keepdims=True), axis=0, keepdims=True)
        for k in (1, 2, 3)
    ]
    start_of = jnp.zeros_like(token)
    for first in firsts:
        start_of = jnp.maximum(start_of, jnp.where(token >= first, first, 0.0))
    prefix = pre_ref[0].astype(F32)
    cache_end = jnp.where(token < firsts[0], prefix - 1.0, -1.0)
    exponent = math.log2(math.e) / math.sqrt(NOPE + ROPE)

    def attend(*parts):
        latent, ropes, seen = [], [], []
        for kind, dx in parts:
            line = wrap(x + dx, SIDE)
            block = kv[pl.ds(line * SIDE, SIDE)].reshape(KEYS, 2 * LAT + 2 * ROPE)
            latent.append(block[:, kind * LAT : (kind + 1) * LAT])
            lane = lax.broadcasted_iota(jnp.int32, (KEYS, 2 * ROPE), 1)
            mine = lane < ROPE if kind == 0 else lane >= ROPE
            ropes.append(jnp.where(mine, block[:, 2 * LAT :], jnp.zeros((), BF16)))
            lane = lax.broadcasted_iota(jnp.int32, (1, KEYS), 1)
            pos = (
                line * (SIDE * CORES * TOK) + (lane // TOK) * (CORES * TOK) + c * TOK + lax.rem(lane, TOK)
            ).astype(F32)
            if kind == 0:
                seen.append(pos <= cache_end)
            else:
                seen.append(jnp.logical_and(pos >= start_of, pos <= token))
        values = jnp.concatenate(latent, axis=0)
        rows_k = jnp.concatenate([values, jnp.concatenate(ropes, axis=0)], axis=1)
        for i, ok in enumerate(seen):
            bias[:, i * KEYS : (i + 1) * KEYS] = jnp.where(ok, 0.0, MASKED)
        for i in range(ROWS // TILE):
            rows = slice(i * TILE, (i + 1) * TILE)
            sc = lax.dot_general(
                qf[rows, :], rows_k, (((1,), (1,)), ((), ())), preferred_element_type=F32
            )
            both = bias[...]
            sc = sc + jnp.concatenate([both] * (TILE // (CORES * TOK)), axis=0)
            m_old = m_ref[rows, :]
            m_new = jnp.maximum(m_old, jnp.max(sc, axis=1, keepdims=True))
            shrink = jnp.exp2((m_old - m_new) * exponent)
            p = jnp.exp2((sc - jnp.concatenate([m_new] * 4, axis=1)) * exponent)
            l_ref[rows, :] = l_ref[rows, :] * shrink + (
                (p[:, 0:128] + p[:, 128:256]) + (p[:, 256:384] + p[:, 384:512])
            )
            acc[rows, :] = acc[rows, :] * jnp.concatenate([shrink] * 4, axis=1) + jnp.dot(
                p.astype(BF16), values, preferred_element_type=F32
            )
            m_ref[rows, :] = m_new

    early = x < 2
    late = jnp.logical_not(early)

    keys.follow(0, NEAR_1)
    hear(0)
    tell(1)
    weights_step(0)
    keys.follow(0, NEAR_2)
    weights_step(1)
    keys.wait(0, 5)

    @pl.when(early)
    def _():
        attend((0, 0), (1, 0))

    hear(1)
    tell(2)
    keys.follow(0, NEAR_3)
    weights_step(2)
    keys.wait(0, 26, 27, 28, 29)

    @pl.when(early)
    def _():
        attend((0, 3), (0, 1))

    @pl.when(late)
    def _():
        attend((1, 0), (1, 3))

    keys.wait(0, 6, 20, 21, 22, 23, 24, 25, 30, 31)

    @pl.when(early)
    def _():
        attend((0, 2), (1, 3))

    @pl.when(late)
    def _():
        attend((1, 2), (1, 1))

    weights_step(3)
    hear(2)

    copies[6].wait()
    half = lax.broadcasted_iota(jnp.int32, (CORES * TOK, 128), 1) < 64
    swaps = []
    for t in range(4):
        for h in (2 * t, 2 * t + 1):
            rows = slice(h * CORES * TOK, (h + 1) * CORES * TOK)
            total = jnp.sum(l_ref[rows, :], axis=1, keepdims=True)
            o = (acc[rows, :] / jnp.where(total > 0.0, total, 1.0)).astype(BF16)
            ph = jnp.dot(o, vup[h], preferred_element_type=F32)
            pp[:, h, :, 0:VD] = ph.reshape(CORES, TOK, VD)
            pp[:, h, :, VD:] = jnp.where(half, m_ref[rows, :], total).reshape(CORES, TOK, 128)
        swap = to_sibling(pp.at[1 - c, pl.ds(2 * t, 2)], pr.at[pl.ds(2 * t, 2)], 2 + t)
        swap.start()
        swaps.append(swap)
    def dealt(g, d):
        to = wrap(z + d, DEPTH)
        return pltpu.make_async_remote_copy(
            src_ref=s1.at[g, to], dst_ref=r1.at[g, z], send_sem=s1s.at[g * DEPTH + d], recv_sem=s1r.at[g * DEPTH + z],
            device_id=(s, to), device_id_type=MESH,
        )

    def landed(src, dst, sem):
        pltpu.make_async_remote_copy(
            src_ref=src, dst_ref=dst, send_sem=s1s.at[0], recv_sem=sem, device_id=up, device_id_type=MESH
        ).wait_recv()

    far_first = (4, 3, 5, 2, 6, 1, 7)
    wide = HEADS * VD // 2
    for g in range(2):
        merged = []
        for t in (2 * g, 2 * g + 1):
            swaps[t].wait_recv()
            for h in (2 * t, 2 * t + 1):
                own, other = pp[c, h], pr[h]
                m0, m1 = own[:, VD : VD + 1], other[:, VD : VD + 1]
                l0, l1 = own[:, VD + 64 : VD + 65], other[:, VD + 64 : VD + 65]
                top = jnp.maximum(m0, m1)
                w0 = l0 * jnp.exp2((m0 - top) * exponent)
                w1 = l1 * jnp.exp2((m1 - top) * exponent)
                norm = w0 + w1
                merged.append(own[:, 0:VD] * (w0 / norm) + other[:, 0:VD] * (w1 / norm))
        left = jnp.concatenate(merged[:2], axis=1)
        right = jnp.concatenate(merged[2:], axis=1)
        for p in range(DEPTH):
            rows = slice(8 * p, 8 * p + 8)
            s1[g, p] = jnp.concatenate([left[rows], right[rows]], axis=0).astype(BF16)
        for d in far_first:
            dealt(g, d).start()
        r1[g, z] = s1[g, z]
    weights_step(4)

    heads = Gather(pha, g2s, g2r, LINES, [(0, wide), (wide, wide)])
    for g in range(2):
        for d in reversed(far_first):
            plane = wrap(z + d, DEPTH)
            landed(s1.at[0, 0], r1.at[g, plane], s1r.at[g * DEPTH + plane])
        blocks = []
        for p in range(DEPTH):
            rows = r1[g, p].astype(F32)
            blocks.append(jnp.concatenate([rows[0:8], rows[8:16]], axis=1))
        pha[chip, :, g * wide : (g + 1) * wide] = jnp.concatenate(blocks, axis=0).astype(BF16)
        heads.start(g, 4, 5, 0, 1, 2, 3)
    weights_step(5)
    for g in range(2):
        heads.follow(g, LINES_1)
    weights_step(6)
    for d in range(DEPTH):
        pass_block(d, 1 - c).wait_recv()

    even = lax.rem(lax.broadcasted_iota(jnp.int32, (COLS, CHIPS * 16), 1), 16) < 8
    sums = [[None, None], [None, None]]
    for g in range(2):
        heads.wait(g, *range(6, 24))
        lanes = slice(g * wide, (g + 1) * wide)
        for i in range(CORES):
            for parity in range(2):
                total = sums[i][parity]
                for p in range(DEPTH // 2):
                    rows = pha[:, 16 * p : 16 * p + 16, lanes].reshape(CHIPS * 16, wide)
                    v = lax.dot_general(
                        wz[2 * p + parity, i, :, lanes], rows, (((1,), (1,)), ((), ())),
                        preferred_element_type=F32,
                    )
                    total = v if total is None else total + v
                sums[i][parity] = total
    products = [jnp.where(even, *pair).T for pair in sums]
    for g in range(CHIPS):
        s4[g] = jnp.concatenate(
            [v[16 * g : 16 * g + 8] + v[16 * g + 8 : 16 * g + 16] for v in products], axis=0
        ).astype(BF16)

    others = [(dx, dy) for dx in (2, 1, 3, 0) for dy in (2, 1, 3, 0)][:-1]

    def over(dx, dy):
        return pltpu.make_async_remote_copy(
            src_ref=s4.at[at(dx, dy)], dst_ref=r4.at[chip], send_sem=s4s.at[dx * SIDE + dy], recv_sem=s4r.at[chip],
            device_id=device(dx, dy), device_id_type=MESH,
        )

    def along(d):
        plane = wrap(z + d, DEPTH)
        return pltpu.make_async_remote_copy(
            src_ref=r4.at[pl.ds(2 * plane, 2)], dst_ref=r5.at[z], send_sem=s5s.at[d], recv_sem=s5r.at[z],
            device_id=(s, plane), device_id_type=MESH,
        )

    for dx, dy in others:
        over(dx, dy).start()
    r4[chip] = s4[chip]
    for dx, dy in reversed(others):
        landed(s4.at[0], r4.at[at(dx, dy)], s4r.at[at(dx, dy)])
    for d in far_first:
        along(d).start()
    r5[z] = r4[pl.ds(2 * z, 2)]
    for d in reversed(far_first):
        plane = wrap(z + d, DEPTH)
        landed(r4.at[pl.ds(0, 2)], r5.at[plane], s5r.at[plane])
    columns = []
    for a in range(2):
        for i in range(CORES):
            columns.append(
                jnp.concatenate([r5[p, a].astype(F32)[8 * i : 8 * i + 8] for p in range(DEPTH)], axis=0)
            )
    out_ref[...] = jnp.concatenate(columns, axis=1).astype(BF16)

    keys.done()
    heads.done()
    q_swap.wait_send()
    for i in range(7):
        around(1, i).wait_send()
        around(-1, i).wait_send()
    for d in range(DEPTH):
        pass_block(d, c).wait_send()
    for d in far_first:
        dealt(0, d).wait_send()
        dealt(1, d).wait_send()
        along(d).wait_send()
    for dx, dy in others:
        over(dx, dy).wait_send()
    for t in range(4):
        swaps[t].wait_send()


def on_device(queries, span_latent, cache_latent, segments, prefix_len, w_uk, value_up_weight, w_out):
    hbm = pl.BlockSpec(memory_space=pltpu.HBM)
    dma = pltpu.SemaphoreType.DMA
    return pl.pallas_call(
        kernel,
        out_shape=jax.ShapeDtypeStruct((TOK, CORES * 2 * COLS), BF16),
        in_specs=[hbm] * 8,
        out_specs=pl.BlockSpec(memory_space=pltpu.VMEM),
        scratch_shapes=[
            pltpu.VMEM((HEADS * TOK, NOPE + ROPE), BF16),
            pltpu.VMEM((TOK, LAT + ROPE), BF16),
            pltpu.VMEM((TOK, LAT + ROPE), BF16),
            pltpu.VMEM((CHIPS, CORES * TOK), jnp.int32),
            pltpu.SMEM((1,), jnp.int32),
            pltpu.VMEM((CHIPS, TOK, 2 * LAT + 2 * ROPE), BF16),
            pltpu.VMEM((HEADS * TOK, NOPE + ROPE), BF16),
            pltpu.VMEM((ROWS, LAT + 2 * ROPE), BF16),
            pltpu.VMEM((ROWS, 128), F32),
            pltpu.VMEM((ROWS, 128), F32),
            pltpu.VMEM((ROWS, LAT), F32),
            pltpu.VMEM((CORES * TOK, 2 * KEYS), F32),
            pltpu.VMEM((HEADS, NOPE, LAT), BF16),
            pltpu.VMEM((HEADS, LAT, VD), BF16),
            pltpu.VMEM((DEPTH, CORES, COLS, HEADS * VD), BF16),
            pltpu.VMEM((CORES, HEADS, TOK, 2 * VD), F32),
            pltpu.VMEM((HEADS, TOK, 2 * VD), F32),
            pltpu.VMEM((2, DEPTH, 16, HEADS * VD // 4), BF16),
            pltpu.VMEM((2, DEPTH, 16, HEADS * VD // 4), BF16),
            pltpu.VMEM((CHIPS, TOK, HEADS * VD), BF16),
            pltpu.VMEM((CHIPS, 16, COLS), BF16),
            pltpu.VMEM((CHIPS, 16, COLS), BF16),
            pltpu.VMEM((DEPTH, 2, 16, COLS), BF16),
            dma((32,)), dma((32,)), dma((48,)), dma((48,)),
            dma((8,)), dma((6,)), dma((6,)), dma((7,)), dma((7,)), dma((7,)), dma((7,)), dma((8,)), dma((8,)),
            dma((16,)), dma((16,)), dma((16,)), dma((16,)), dma((8,)), dma((8,)),
            pltpu.SemaphoreType.REGULAR((3,)),
        ],
        compiler_params=pltpu.CompilerParams(
            collective_id=0, has_side_effects=True, vmem_limit_bytes=56 * 1024 * 1024
        ),
        name="prefill",
    )(
        queries.reshape(HEADS * TOK, NOPE + ROPE),
        span_latent,
        cache_latent,
        segments.reshape(CHIPS, CORES * TOK),
        prefix_len,
        w_uk,
        value_up_weight,
        w_out.T,
    )


def solution(mesh):
    placed = (
        P("seq", "head", None),
        P("seq", None),
        P("seq", None),
        P(),
        P(),
        P("head", None, None),
        P("head", None, None),
        P("head", "seq"),
    )
    return jax.shard_map(
        on_device, mesh=mesh, in_specs=placed, out_specs=P("seq", "head"), check_vma=False
    )
```

time: 250 us -> 74.5 us (0.30)
  waiting for transfers between devices: 196 us -> 0 us
  Pallas kernels: 0 us -> 71.8 us
  matrix products: 19.8 us -> 0 us
  between operations: 13.9 us -> 0.66 us
  local copies, waits for them, and re-layouts: 13.3 us -> 1.55 us
  other arithmetic: 6.46 us -> 0 us
    all_gather x3 -> x0, waiting for transfers between devices: 153 us -> none  [the longest x1 59.1 us: on_device(): lax.all_gather(w_out, 'seq', axis=1, tiled=True)]
    pallas_call x0 -> x1, Pallas kernels: none -> 71.8 us  [on_device(): pl.pallas_call(kernel, out_shape=jax.ShapeDtypeStruct((TOK, CORES * 2 * C...]
    unnamed x5 -> x0, waiting for transfers between devices: 43.4 us -> none
    dot_general x5 -> x0, matrix products: 19.8 us -> none  [the longest x1 9.72 us: on_device(): jnp.dot(head_split, lax.all_gather(w_out, 'seq', axis=1, tiled=True), pre...]
    unnamed x12 -> x1, local copies, waits for them, and re-layouts: 6.86 us -> 1.55 us
    concatenate x1 -> x0, local copies, waits for them, and re-layouts: 3.51 us -> none  [on_device(): key_rows = jnp.concatenate([cache_portion, span_piece], axis=0)]
    reduce_sum x1 -> x0, other arithmetic: 2.81 us -> none  [on_device(): new_sum = jnp.sum(expo, axis=1)]
    and x1 -> x0, other arithmetic: 2.66 us -> none  [on_device(): (row_segment[:, None] == segments[None, :]) & (key_position[None, :] <= r...]
  transfers between devices with their start and end apart: 4 -> 0, of which waited for: 4 -> 0; matrix products, arithmetic and copies ran while one was open for 11% -> 0% of each run, Pallas kernels for 0% -> 0%
where the time goes in v2:
time: 74.5 us; the launch traced here: 74 us
  Pallas kernels  71.8 us (96%)
  local copies, waits for them, and re-layouts  1.55 us (2%)
    pallas_call x1, Pallas kernels, on_device(): pl.pallas_call(kernel, out_shape=jax.ShapeDtypeStruct((TOK, CORES * 2 * C...  71.8 us
    unnamed x1, local copies, waits for them, and re-layouts  1.55 us

profile of v2, /device:TPU:4, one launch (start us, length us, event | category | flops | bytes accessed | tf_op | source)
XLA Modules:
  0.0 74.0 jit_solution(15854453860049176405)
XLA Ops:
  0.7 71.8 %prefill.1 = bf16[64,896]{1,0:T(8,128)(2,1)} custom-call(bf16[512,192]{1,0:T(8,128)(2,1)} %bitcast.4, bf16[64,576]{1,0:T(8,128)(2,1)} %span_hbm.1, bf16[64,576]{1,0:T(8,128)(2,1)} %cache_hbm.1, s32[16,128]{1,0:T(8,128)} %bitcast.5, s32[1]{0:T(128)S(6)} %copy.10.pre_hbm, bf16[8,128,512]{2,1,0:T(8,128)(2,1)} %wuk_hbm.1, bf16[8,512,128]{2,1,0:T(8,128)(2,1)} %vup_hbm.1, ...), custom_call_target="tpu_custom_call" | custom-call | tf_op jit(solution)/shard_map/prefill/pallas_call | solution.py:493
  72.4 1.6 %copy.11 = bf16[64,896]{1,0:T(8,128)(2,1)} copy(bf16[64,896]{1,0:T(8,128)(2,1)} %prefill.1) | data formatting | bytes 229376

commit v3 on v2

--- a/solution.py
+++ b/solution.py
@@ -183,7 +183,7 @@
     q_swap.start()
 
     def around(way, i):
-        half = i % 2 if i < 6 or way > 0 else 1
+        half = i % 2 if way > 0 else (i + 1) % 2
         block = wrap(z - way * (i // 2) + DEPTH, DEPTH)
         ref = wz.at[block, c, pl.ds(half * (COLS // 2), COLS // 2)]
         send, recv = (wus, wur) if way > 0 else (wds, wdr)
@@ -193,7 +193,7 @@
         )
 
     def around_landed(way, i):
-        half = i % 2 if i < 6 or way > 0 else 1
+        half = i % 2 if way > 0 else (i + 1) % 2
         block = wrap(z - way * (i // 2 + 1) + DEPTH, DEPTH)
         ref = wz.at[block, c, pl.ds(half * (COLS // 2), COLS // 2)]
         send, recv = (wus, wur) if way > 0 else (wds, wdr)
@@ -212,12 +212,8 @@
     def weights_step(i):
         for way in (1, -1):
             around_landed(way, i)
-            if i < 4:
+            if i < 3:
                 around(way, i + 2).start()
-        if i == 4:
-            around(1, 6).start()
-        elif i == 5:
-            around(-1, 6).start()
         if i % 2 == 1:
             pass_block(i // 2 + 1, c).start()
             pass_block(-(i // 2 + 1), c).start()
@@ -341,7 +337,6 @@
     def _():
         attend((1, 2), (1, 1))
 
-    weights_step(3)
     hear(2)
 
     copies[6].wait()
@@ -393,7 +388,6 @@
         for d in far_first:
             dealt(g, d).start()
         r1[g, z] = s1[g, z]
-    weights_step(4)
 
     heads = Gather(pha, g2s, g2r, LINES, [(0, wide), (wide, wide)])
     for g in range(2):
@@ -406,9 +400,21 @@
             blocks.append(jnp.concatenate([rows[0:8], rows[8:16]], axis=1))
         pha[chip, :, g * wide : (g + 1) * wide] = jnp.concatenate(blocks, axis=0).astype(BF16)
         heads.start(g, 4, 5, 0, 1, 2, 3)
-    weights_step(5)
+    weights_step(3)
+    weights_step(4)
+    for i in (5, 6):
+        around(1, i).start()
+        around(-1, i).start()
     for g in range(2):
         heads.follow(g, LINES_1)
+    keys.done()
+    q_swap.wait_send()
+    for t in range(4):
+        swaps[t].wait_send()
+    for d in far_first:
+        dealt(0, d).wait_send()
+        dealt(1, d).wait_send()
+    weights_step(5)
     weights_step(6)
     for d in range(DEPTH):
         pass_block(d, 1 - c).wait_recv()
@@ -453,11 +459,19 @@
     for dx, dy in others:
         over(dx, dy).start()
     r4[chip] = s4[chip]
+    heads.done()
+    for i in range(7):
+        around(1, i).wait_send()
+        around(-1, i).wait_send()
+    for d in range(DEPTH):
+        pass_block(d, c).wait_send()
     for dx, dy in reversed(others):
         landed(s4.at[0], r4.at[at(dx, dy)], s4r.at[at(dx, dy)])
     for d in far_first:
         along(d).start()
     r5[z] = r4[pl.ds(2 * z, 2)]
+    for dx, dy in others:
+        over(dx, dy).wait_send()
     for d in reversed(far_first):
         plane = wrap(z + d, DEPTH)
         landed(r4.at[pl.ds(0, 2)], r5.at[plane], s5r.at[plane])
@@ -469,22 +483,8 @@
             )
     out_ref[...] = jnp.concatenate(columns, axis=1).astype(BF16)
 
-    keys.done()
-    heads.done()
-    q_swap.wait_send()
-    for i in range(7):
-        around(1, i).wait_send()
-        around(-1, i).wait_send()
-    for d in range(DEPTH):
-        pass_block(d, c).wait_send()
     for d in far_first:
-        dealt(0, d).wait_send()
-        dealt(1, d).wait_send()
         along(d).wait_send()
-    for dx, dy in others:
-        over(dx, dy).wait_send()
-    for t in range(4):
-        swaps[t].wait_send()
 
 
 def on_device(queries, span_latent, cache_latent, segments, prefix_len, w_uk, value_up_weight, w_out):

time: 74.5 us -> 69.8 us (0.937)
  Pallas kernels: 71.8 us -> 67 us
    pallas_call x1, Pallas kernels: 71.8 us -> 67 us  [on_device(): pl.pallas_call(kernel, out_shape=jax.ShapeDtypeStruct((TOK, CORES * 2 * C...]
where the time goes in v3:
time: 69.8 us; the launch traced here: 69.3 us
  Pallas kernels  67 us (96%)
  local copies, waits for them, and re-layouts  1.55 us (2%)
    pallas_call x1, Pallas kernels, on_device(): pl.pallas_call(kernel, out_shape=jax.ShapeDtypeStruct((TOK, CORES * 2 * C...  67 us
    unnamed x1, local copies, waits for them, and re-layouts  1.55 us

profile of v3, /device:TPU:4, one launch (start us, length us, event | category | flops | bytes accessed | tf_op | source)
XLA Modules:
  0.0 69.3 jit_solution(14433990655213699984)
XLA Ops:
  0.7 67.0 %prefill.1 = bf16[64,896]{1,0:T(8,128)(2,1)} custom-call(bf16[512,192]{1,0:T(8,128)(2,1)} %bitcast.4, bf16[64,576]{1,0:T(8,128)(2,1)} %span_hbm.1, bf16[64,576]{1,0:T(8,128)(2,1)} %cache_hbm.1, s32[16,128]{1,0:T(8,128)} %bitcast.5, s32[1]{0:T(128)S(6)} %copy.10.pre_hbm, bf16[8,128,512]{2,1,0:T(8,128)(2,1)} %wuk_hbm.1, bf16[8,512,128]{2,1,0:T(8,128)(2,1)} %vup_hbm.1, ...), custom_call_target="tpu_custom_call" | custom-call | tf_op jit(solution)/shard_map/prefill/pallas_call | solution.py:493
  67.7 1.6 %copy.11 = bf16[64,896]{1,0:T(8,128)(2,1)} copy(bf16[64,896]{1,0:T(8,128)(2,1)} %prefill.1) | data formatting | bytes 229376

commit v4 on v3

--- a/solution.py
+++ b/solution.py
@@ -346,7 +346,7 @@
         for h in (2 * t, 2 * t + 1):
             rows = slice(h * CORES * TOK, (h + 1) * CORES * TOK)
             total = jnp.sum(l_ref[rows, :], axis=1, keepdims=True)
-            o = (acc[rows, :] / jnp.where(total > 0.0, total, 1.0)).astype(BF16)
+            o = (acc[rows, :] * (1.0 / jnp.where(total > 0.0, total, 1.0))).astype(BF16)
             ph = jnp.dot(o, vup[h], preferred_element_type=F32)
             pp[:, h, :, 0:VD] = ph.reshape(CORES, TOK, VD)
             pp[:, h, :, VD:] = jnp.where(half, m_ref[rows, :], total).reshape(CORES, TOK, 128)

time: 69.8 us -> 69.8 us (level)
  no operation moved by 1% of the time
where the time goes in v4:
time: 69.8 us; the launch traced here: 69.3 us
  Pallas kernels  67 us (96%)
  local copies, waits for them, and re-layouts  1.55 us (2%)
    pallas_call x1, Pallas kernels, on_device(): pl.pallas_call(kernel, out_shape=jax.ShapeDtypeStruct((TOK, CORES * 2 * C...  67 us
    unnamed x1, local copies, waits for them, and re-layouts  1.55 us

profile of v4, /device:TPU:4, one launch (start us, length us, event | category | flops | bytes accessed | tf_op | source)
XLA Modules:
  0.0 69.3 jit_solution(14433990655213699984)
XLA Ops:
  0.7 67.0 %prefill.1 = bf16[64,896]{1,0:T(8,128)(2,1)} custom-call(bf16[512,192]{1,0:T(8,128)(2,1)} %bitcast.4, bf16[64,576]{1,0:T(8,128)(2,1)} %span_hbm.1, bf16[64,576]{1,0:T(8,128)(2,1)} %cache_hbm.1, s32[16,128]{1,0:T(8,128)} %bitcast.5, s32[1]{0:T(128)S(6)} %copy.10.pre_hbm, bf16[8,128,512]{2,1,0:T(8,128)(2,1)} %wuk_hbm.1, bf16[8,512,128]{2,1,0:T(8,128)(2,1)} %vup_hbm.1, ...), custom_call_target="tpu_custom_call" | custom-call | tf_op jit(solution)/shard_map/prefill/pallas_call | solution.py:493
  67.7 1.6 %copy.11 = bf16[64,896]{1,0:T(8,128)(2,1)} copy(bf16[64,896]{1,0:T(8,128)(2,1)} %prefill.1) | data formatting | bytes 229376
